TPU v7x, 32 devices: a whole 2x2x4 slice. The times are simulated.
32 devices in a mesh: vox: 8 (over z, y), opt: 4 (over x, core).
Axes of the slice: x: 2, y: 2, z: 4, core: 2. Of those that a mesh axis runs over, the one named last changes fastest.
Arguments:
- source_fields: bfloat16 [1024, 6144], P('opt', 'vox'), may hold values from -6 to 6
- detector_fields: bfloat16 [4096, 6144], P('opt', 'vox'), may hold values from -6 to 6
- measured: float32 [1024, 4096], P('vox', 'opt'), may hold values from -6 to 6
- valid_pair: int32 [1024, 4096], P('vox', 'opt'), may hold values 0 or 1
- weight_class: int32 [1024, 4096], P('vox', 'opt'), may hold values from 0 to 3
- absorption: float32 [6144], P('vox'), may hold values from 0 to 1
Outputs:
- absorption_out: float32 [6144], P('vox')
- residual_out: float32 [1024, 4096], P('vox', 'opt')
All inputs are finite; a program needn't handle non-finite values. No bound on the sum of `valid_pair` on one device may be relied on, other than what follows from the above.
Results may differ from a plain program's by a relative error of at most 0.0026.
Values may be sent and summed in bfloat16 or wider, within the bound.
A program may use at most 64 MiB of HBM per device.

v0:
```python
import jax
import jax.numpy as jnp
from jax import lax
from jax.sharding import PartitionSpec as P

NS = 1024
ND = 4096
ITERS = 2


def local(source_fields, detector_fields, measured, valid_pair, weight_class, absorption):
    vox_count = lax.axis_size("vox")
    voxels = absorption.shape[0] * vox_count
    pred_scale = 1.0 / jnp.sqrt(jnp.float32(voxels))
    grad_scale = jnp.sqrt(jnp.float32(voxels)) / (jnp.float32(NS) * jnp.float32(ND))
    maskf = valid_pair.astype(jnp.float32) / (1.0 + weight_class.astype(jnp.float32))
    mu_now = absorption
    weighted = jnp.zeros(measured.shape, jnp.float32)
    for step in range(ITERS):
        scaled = (detector_fields * mu_now[None, :]).astype(jnp.bfloat16)
        partial_pred = lax.dot_general(
            lax.all_gather(source_fields, "opt", axis=0, tiled=True),
            scaled,
            (((1,), (1,)), ((), ())),
            preferred_element_type=jnp.float32,
        )
        predicted = lax.psum_scatter(partial_pred, "vox", scatter_dimension=0, tiled=True)
        weighted = maskf * (predicted * pred_scale - measured)
        weighted_b = weighted.astype(jnp.bfloat16)
        inner = jnp.dot(
            lax.all_gather(weighted_b, "vox", axis=0, tiled=True),
            detector_fields,
            preferred_element_type=jnp.float32,
        )
        local_grad = jnp.sum(
            inner * lax.all_gather(source_fields, "opt", axis=0, tiled=True), axis=0
        )
        gradient = lax.psum(local_grad, "opt") * grad_scale
        mu_now = jnp.maximum(mu_now - 2.0 * gradient, 0.0)
    return (mu_now, weighted)


def solution(mesh):
    placed = (
        P("opt", "vox"),
        P("opt", "vox"),
        P("vox", "opt"),
        P("vox", "opt"),
        P("vox", "opt"),
        P("vox"),
    )
    return jax.shard_map(
        local, mesh=mesh, in_specs=placed, out_specs=(P("vox"), P("vox", "opt")), check_vma=False
    )
```

profile of v0, /device:TPU:0, one launch (start us, length us, event | category | flops | bytes accessed | tf_op | source)
XLA Modules:
  0.0 352.4 jit_solution(14834758548979009988)
XLA Ops:
  7.2 0.7 all-gather.4.cloned.1.call-update
  7.9 0.0 reduce-scatter.3.cloned.1.call-start
  7.9 24.0 %all-gather.4.cloned.1.call-done = bf16[1024,768]{1,0:T(8,128)(2,1)} async-done(((bf16[256,768]{1,0:T(8,128)(2,1)}), bf16[1024,768]{1,0:T(8,128)(2,1)}) %all-gather.4.cloned.1.call-update) | async-done | bytes 1572880 | tf_op jit(solution)/shard_map/all_gather | solution.py:22
  31.9 5.7 %convolution_bitcast_fusion.1 = f32[1024,1024]{0,1:T(8,128)} fusion(bf16[1024,768]{1,0:T(8,128)(2,1)} %all-gather.4.cloned.1.call-done, bf16[1024,768]{1,0:T(8,128)(2,1)} %param.7, f32[768]{0:T(1024)} %param.11), kind=kOutput, calls=%fused_computation.9 | convolution fusion | flops 1612972032 | bytes 7343104 | tf_op jit(solution)/shard_map/dot_general | solution.py:21
  37.7 0.0 all-gather.6.cloned.1.call-start
  37.7 1.0 copy-done
  38.7 0.2 copy.10
  38.9 0.2 copy.8
  39.1 0.2 copy.9
  39.3 87.0 %reduce-scatter.3.cloned.1.call-done = f32[128,1024]{0,1:T(8,128)} async-done(((f32[1024,1024]{0,1:T(8,128)}), f32[128,1024]{0,1:T(8,128)}) %reduce-scatter.3.cloned.1.call-update) | async-done | bytes 524304 | tf_op jit(solution)/shard_map/reduce_scatter | solution.py:27
  126.3 1.9 multiply_convert_fusion
  128.2 0.0 reduce-scatter.5.cloned.1.call-start
  128.3 51.7 %all-gather.6.cloned.1.call-done = bf16[1024,1024]{0,1:T(8,128)(2,1)} async-done(((bf16[128,1024]{0,1:T(8,128)(2,1)}), bf16[1024,1024]{0,1:T(8,128)(2,1)}) %all-gather.6.cloned.1.call-update) | async-done | bytes 2097168 | tf_op jit(solution)/shard_map/all_gather | solution.py:31
  179.9 3.9 %fusion.2 = f32[768]{0:T(1024)S(1)} fusion(bf16[1024,768]{1,0:T(8,128)(2,1)} %all-gather.4.cloned.1.call-done, bf16[1024,1024]{0,1:T(8,128)(2,1)} %all-gather.6.cloned.1.call-done, bf16[1024,768]{1,0:T(8,128)(2,1)S(1)} %copy-done.4), kind=kOutput, calls=%fused_computation.6 | convolution fusion | flops 1612971264 | bytes 5245952 | tf_op jit(solution)/shard_map/dot_general | solution.py:30
  183.9 6.2 %psum.14 = f32[768]{0:T(1024)S(1)} all-reduce(f32[768]{0:T(1024)S(1)} %fusion.2), channel_id=1, replica_groups=mesh['vox'=8,'opt'=4] {'opt'}, use_global_device_ids=true, to_apply=%region_2.0 | all-reduce | flops 768 | bytes 6144 | tf_op jit(solution)/shard_map/psum | solution.py:38
  190.0 5.2 %convolution_bitcast_fusion = f32[1024,1024]{0,1:T(8,128)} fusion(bf16[1024,768]{1,0:T(8,128)(2,1)} %all-gather.4.cloned.1.call-done, bf16[1024,768]{1,0:T(8,128)(2,1)S(1)} %copy-done.4, f32[768]{0:T(1024)S(1)} %subtract_maximum_fusion.1), kind=kOutput, calls=%fused_computation.8 | convolution fusion | flops 1612972032 | bytes 7343104 | tf_op jit(solution)/shard_map/dot_general | solution.py:21
  195.3 0.0 all-gather.8.cloned.1.call-start
  195.3 86.5 %reduce-scatter.5.cloned.1.call-done = f32[128,1024]{0,1:T(8,128)} async-done(((f32[1024,1024]{0,1:T(8,128)}), f32[128,1024]{0,1:T(8,128)}) %reduce-scatter.5.cloned.1.call-update) | async-done | bytes 524304 | tf_op jit(solution)/shard_map/reduce_scatter | solution.py:27
  281.8 1.9 fusion.8
  283.8 1.0 copy.12
  284.8 50.0 %all-gather.8.cloned.1.call-done = bf16[1024,1024]{0,1:T(8,128)(2,1)} async-done(((bf16[128,1024]{0,1:T(8,128)(2,1)}), bf16[1024,1024]{0,1:T(8,128)(2,1)}) %all-gather.8.cloned.1.call-update) | async-done | bytes 2097168 | tf_op jit(solution)/shard_map/all_gather | solution.py:31
  334.7 4.4 %fusion.3 = f32[768]{0:T(1024)S(1)} fusion(bf16[1024,768]{1,0:T(8,128)(2,1)} %all-gather.4.cloned.1.call-done, bf16[1024,1024]{0,1:T(8,128)(2,1)} %all-gather.8.cloned.1.call-done, bf16[1024,768]{1,0:T(8,128)(2,1)} %param.7), kind=kOutput, calls=%fused_computation.7 | convolution fusion | flops 1612971264 | bytes 5245952 | tf_op jit(solution)/shard_map/dot_general | solution.py:30
  339.1 6.2 %psum.15 = f32[768]{0:T(1024)S(1)} all-reduce(f32[768]{0:T(1024)S(1)} %fusion.3), channel_id=1, replica_groups=mesh['vox'=8,'opt'=4] {'opt'}, use_global_device_ids=true, to_apply=%region_5.0 | all-reduce | flops 768 | bytes 6144 | tf_op jit(solution)/shard_map/psum | solution.py:38
  345.3 0.6 subtract_maximum_fusion
  (15 shorter events, 0.1 us)
Async XLA Ops:
  7.2 24.8 %all-gather.4.cloned.1.call-start = ((), (), s32[]{:S(2)}) async-start(), calls=%async_computation.2 | async-start | bytes 1966080 | tf_op jit(solution)/shard_map/all_gather | solution.py:22
  7.9 118.4 %reduce-scatter.3.cloned.1.call-start = ((), (), s32[]{:S(2)}) async-start(), calls=%async_computation.3 | async-start | bytes 4718592 | tf_op jit(solution)/shard_map/reduce_scatter | solution.py:27
  37.6 1.0 copy-start
  37.6 1.2 copy-start.1
  37.6 1.4 copy-start.2
  37.7 142.3 %all-gather.6.cloned.1.call-start = ((), (), s32[]{:S(2)}) async-start(), calls=%async_computation.4 | async-start | bytes 2359296 | tf_op jit(solution)/shard_map/all_gather | solution.py:31
  39.3 140.7 %copy-start.4 = (bf16[1024,768]{1,0:T(8,128)(2,1)S(1)}, bf16[1024,768]{1,0:T(8,128)(2,1)}, u32[]{:S(2)}) copy-start(bf16[1024,768]{1,0:T(8,128)(2,1)} %param.7) | copy-start | bytes 4718596
  128.2 61.9 %copy-start.3 = (f32[768]{0:T(1024)S(1)}, f32[768]{0:T(1024)}, u32[]{:S(2)}) copy-start(f32[768]{0:T(1024)} %param.11) | copy-start | bytes 9220
  128.2 153.6 %reduce-scatter.5.cloned.1.call-start = ((), (), s32[]{:S(2)}) async-start(), calls=%async_computation.5 | async-start | bytes 4718592 | tf_op jit(solution)/shard_map/reduce_scatter | solution.py:27
  195.3 139.5 %all-gather.8.cloned.1.call-start = ((), (), s32[]{:S(2)}) async-start(), calls=%async_computation.6 | async-start | bytes 2359296 | tf_op jit(solution)/shard_map/all_gather | solution.py:31
Sparse Core Ops, SparseCore 0:
  9.6 22.3 all-gather.3
  37.8 88.4 reduce-scatter.2
  129.1 50.8 all-gather.5
  195.4 86.4 reduce-scatter.4
  283.9 50.8 all-gather.7
where the time goes:
time: 353 us; the launch traced here: 352 us
  waiting for transfers between devices  300 us (85%)
  matrix products  19.2 us (5%)
  between operations  13.9 us (4%)
  blocking collectives  12.3 us (3%)
  other arithmetic  4.42 us (1%)
    reduce_scatter x2, waiting for transfers between devices, local(): lax.psum_scatter(partial_pred, 'vox', scatter_dimension=0, tiled=True)  174 us
    all_gather x2, waiting for transfers between devices, local(): lax.all_gather(weighted_b, 'vox', axis=0, tiled=True)  102 us
    all_gather x1, waiting for transfers between devices, local(): lax.all_gather(source_fields, 'opt', axis=0, tiled=True)  24 us
    psum x2, blocking collectives, local(): gradient = lax.psum(local_grad, 'opt') * grad_scale  12.3 us
    dot_general x2, matrix products, local(): lax.dot_general(lax.all_gather(source_fields, 'opt', axis=0, tiled=True),...  10.8 us
    dot_general x2, matrix products, local(): jnp.dot(lax.all_gather(weighted_b, 'vox', axis=0, tiled=True), detector_f...  8.32 us
  transfers between devices with their start and end apart: 5, of which 5 were waited for; matrix products, arithmetic and copies ran while one was open for 0% of the time, Pallas kernels for 0%

commit v1 on v0

v1 whole, which is shorter than its diff:
```python
import functools

import jax
import jax.numpy as jnp
import numpy as np
from jax import lax
from jax.experimental import pallas as pl
from jax.experimental.pallas import tpu as pltpu
from jax.sharding import PartitionSpec as P

ITERS = 2
MESH = pl.DeviceIdType.MESH


def kernel(
    A, B, NO, C, pred_scale, grad_scale,
    s_ref, d_ref, meas_ref, valid_ref, class_ref, mu_in,
    mu_ref, res_ref,
    s_full, maskf, scaled, ysend, yrecv, own, zsend, zrecv, wfull, gbuf,
    sx_send, sx_recv, sc_send, sc_recv, y_send, y_recv, z_send, z_recv,
    wz_send, wz_recv, wy_send, wy_recv, g_send, g_recv,
):
    q, R, X = s_ref.shape
    W = d_ref.shape[0] // C
    vox = lax.axis_index("vox")
    opt = lax.axis_index("opt")
    z, y = vox // B, lax.rem(vox, B)
    chip, core = opt // 2, lax.rem(opt, 2)
    NC = NO // 2
    mate = chip * 2 + 1 - core
    y_peers = [lax.rem(y + k, B) for k in range(1, B)]
    z_peers = [lax.rem(z + k, A) for k in range(1, A)]
    o_peers = [lax.rem(opt + k, NO) for k in range(1, NO)]
    c_peers = [lax.rem(chip + k, NC) for k in range(1, NC)]

    def at(zz, yy):
        return {"vox": zz * B + yy}

    barrier = pltpu.get_barrier_semaphore()
    for p in y_peers:
        pl.semaphore_signal(barrier, inc=1, device_id=at(z, p), device_id_type=MESH)
    for p in z_peers:
        pl.semaphore_signal(barrier, inc=1, device_id=at(p, y), device_id_type=MESH)
    for p in o_peers:
        pl.semaphore_signal(barrier, inc=1, device_id={"opt": p}, device_id_type=MESH)
    pl.semaphore_wait(barrier, A - 1 + B - 1 + NO - 1)

    def remote(src, dst, send, recv, where):
        return pltpu.make_async_remote_copy(
            src_ref=src, dst_ref=dst, send_sem=send, recv_sem=recv,
            device_id=where, device_id_type=MESH,
        )

    def block(j):
        return s_full.at[pl.ds(j * q, q)]

    def to_chip(p, j):
        return remote(s_ref, block(j), sx_send.at[p], sx_recv.at[j], {"opt": p * 2 + core})

    def to_mate(src, j):
        return remote(src, block(j), sc_send.at[j], sc_recv.at[j], {"opt": mate})

    for p in c_peers:
        to_chip(p, opt).start()
    to_mate(s_ref, opt).start()
    s_full[pl.ds(opt * q, q)] = s_ref[...]
    mu_ref[...] = mu_in[...]
    maskf[...] = valid_ref[...].astype(jnp.float32) / (1.0 + class_ref[...].astype(jnp.float32))
    for p in c_peers:
        to_chip(p, p * 2 + core).wait_recv()
        to_mate(block(p * 2 + core), p * 2 + core).start()
    for p in range(NC):
        to_mate(s_ref, p * 2 + 1 - core).wait_recv()
    for p in c_peers:
        to_chip(p, opt).wait_send()
        to_mate(s_ref, p * 2 + core).wait_send()
    to_mate(s_ref, opt).wait_send()

    def step(it, carry):
        def y_copy(c, p):
            return remote(
                ysend.at[c, p], yrecv.at[it, c, y], y_send.at[c, p], y_recv.at[it, c, y], at(z, p)
            )

        def z_copy(c, t, src):
            return remote(
                zsend.at[c, t], zrecv.at[it, c, src], z_send.at[c, t], z_recv.at[it, c, src], at(t, y)
            )

        def wz_copy(c, t, src):
            mine = wfull.at[it, c, src * B + y]
            return remote(mine, mine, wz_send.at[c, t], wz_recv.at[it, c, src], at(t, y))

        def wy_copy(c, src, p, yy):
            mine = wfull.at[it, c, src * B + yy]
            return remote(mine, mine, wy_send.at[c, src, p], wy_recv.at[it, c, src, yy], at(z, p))

        def rows_of(yy):
            return jnp.concatenate([s_full[a * B + yy] for a in range(A)], axis=0)

        def predict(c):
            scaled[...] = (
                d_ref[pl.ds(c * W, W)].astype(jnp.float32) * mu_ref[...]
            ).astype(jnp.bfloat16)

            def part(yy):
                return lax.dot_general(
                    rows_of(yy), scaled[...], (((1,), (1,)), ((), ())),
                    preferred_element_type=jnp.float32,
                ).reshape(A, R, W)

            for p in y_peers:
                ysend[c, p] = part(p).astype(jnp.bfloat16)
                y_copy(c, p).start()
            own[c] = part(y)

        def over_y(c):
            for p in y_peers:
                remote(
                    ysend.at[c, p], yrecv.at[it, c, p], y_send.at[c, p], y_recv.at[it, c, p], at(z, p)
                ).wait_recv()
            for t in z_peers:
                total = own[c, t]
                for p in y_peers:
                    total = total + yrecv[it, c, p, t].astype(jnp.float32)
                zsend[c, t] = total.astype(jnp.bfloat16)
                z_copy(c, t, z).start()

        def over_z(c):
            total = own[c, z]
            for p in y_peers:
                total = total + yrecv[it, c, p, z].astype(jnp.float32)
            for t in z_peers:
                z_copy(c, t, t).wait_recv()
                total = total + zrecv[it, c, t].astype(jnp.float32)
            cols = pl.ds(c * W, W)
            weighted = maskf[:, cols] * (total * pred_scale - meas_ref[:, cols])
            res_ref[:, cols] = weighted
            wfull[it, c, vox] = weighted.astype(jnp.bfloat16)
            for p in y_peers:
                wy_copy(c, z, p, y).start()
            for t in z_peers:
                wz_copy(c, t, z).start()

        def forward(c):
            for t in z_peers:
                wz_copy(c, t, t).wait_recv()
                for p in y_peers:
                    wy_copy(c, t, p, y).start()

        def gradient(c, total):
            for t in range(A):
                for p in y_peers:
                    wy_copy(c, t, p, p).wait_recv()
            d = d_ref[pl.ds(c * W, W)]

            def rows(a, total):
                w = wfull[it, c, pl.ds(a * B, B)].reshape(B * R, W)
                s = s_full[pl.ds(a * B, B)].reshape(B * R, X).astype(jnp.float32)
                inner = jnp.dot(w, d, preferred_element_type=jnp.float32) * s
                return total + jnp.sum(inner.reshape(B * R // 8, 8, X), axis=0)

            return lax.fori_loop(0, A, rows, total)

        for c in range(C):
            predict(c)
        total = jnp.zeros((8, X), jnp.float32)
        for slot in range(C + 4):
            if slot < C:
                over_y(slot)
            if 0 <= slot - 1 < C:
                over_z(slot - 1)
            if 0 <= slot - 2 < C:
                forward(slot - 2)
            if 0 <= slot - 3 < C:
                total = gradient(slot - 3, total)

        def g_copy(p, src):
            mine = gbuf.at[it, src]
            return remote(mine, mine, g_send.at[p], g_recv.at[it, src], {"opt": p})

        gbuf[it, opt] = total
        for p in o_peers:
            g_copy(p, opt).start()
        for c in range(C):
            for p in y_peers:
                y_copy(c, p).wait_send()
                for t in range(A):
                    wy_copy(c, t, p, y).wait_send()
            for t in z_peers:
                z_copy(c, t, z).wait_send()
                wz_copy(c, t, z).wait_send()
        for p in o_peers:
            g_copy(p, p).wait_recv()
        total = gbuf[it, 0]
        for j in range(1, NO):
            total = total + gbuf[it, j]
        grad = jnp.sum(total, axis=0, keepdims=True) * grad_scale
        mu_ref[...] = jnp.maximum(mu_ref[...] - 2.0 * grad, 0.0)
        for p in o_peers:
            g_copy(p, opt).wait_send()
        return carry

    lax.fori_loop(0, ITERS, step, 0)


def local(source_fields, detector_fields, measured, valid_pair, weight_class, absorption):
    NV, NO = lax.axis_size("vox"), lax.axis_size("opt")
    R, DL = measured.shape
    X = absorption.shape[0]
    q = source_fields.shape[0] // R
    B = 2
    A = NV // B
    W = min(DL, 256)
    C = DL // W
    pred_scale = float(np.float32(1.0) / np.sqrt(np.float32(X * NV)))
    grad_scale = float(np.sqrt(np.float32(X * NV)) / np.float32(R * NV * DL * NO))
    bf, f32 = jnp.bfloat16, jnp.float32
    dma = pltpu.SemaphoreType.DMA
    vmem = pl.BlockSpec(memory_space=pltpu.VMEM)
    mu, weighted = pl.pallas_call(
        functools.partial(kernel, A, B, NO, C, pred_scale, grad_scale),
        out_shape=(
            jax.ShapeDtypeStruct((1, X), f32),
            jax.ShapeDtypeStruct((R, DL), f32),
        ),
        in_specs=[vmem] * 6,
        out_specs=(vmem, vmem),
        scratch_shapes=[
            pltpu.VMEM((A * B, R, X), bf),
            pltpu.VMEM((R, DL), f32),
            pltpu.VMEM((W, X), bf),
            pltpu.VMEM((C, B, A, R, W), bf),
            pltpu.VMEM((ITERS, C, B, A, R, W), bf),
            pltpu.VMEM((C, A, R, W), f32),
            pltpu.VMEM((C, A, R, W), bf),
            pltpu.VMEM((ITERS, C, A, R, W), bf),
            pltpu.VMEM((ITERS, C, A * B, R, W), bf),
            pltpu.VMEM((ITERS, NO, 8, X), f32),
            dma((NO // 2,)), dma((NO,)), dma((NO,)), dma((NO,)),
            dma((C, B)), dma((ITERS, C, B)),
            dma((C, A)), dma((ITERS, C, A)),
            dma((C, A)), dma((ITERS, C, A)),
            dma((C, A, B)), dma((ITERS, C, A, B)),
            dma((NO,)), dma((ITERS, NO)),
        ],
        compiler_params=pltpu.CompilerParams(
            collective_id=0, has_side_effects=True, vmem_limit_bytes=52 * 1024 * 1024
        ),
    )(
        source_fields.reshape(q, R, X), detector_fields, measured, valid_pair, weight_class,
        absorption.reshape(1, X),
    )
    return mu.reshape(X), weighted


def solution(mesh):
    placed = (
        P("opt", "vox"),
        P("opt", "vox"),
        P("vox", "opt"),
        P("vox", "opt"),
        P("vox", "opt"),
        P("vox"),
    )
    return jax.shard_map(
        local, mesh=mesh, in_specs=placed, out_specs=(P("vox"), P("vox", "opt")), check_vma=False
    )
```

time: 353 us -> 154 us (0.44)
  waiting for transfers between devices: 300 us -> 0 us
  Pallas kernels: 0 us -> 147 us
  matrix products: 19.2 us -> 0 us
  between operations: 13.9 us -> 0.64 us
  blocking collectives: 12.3 us -> 0 us
  other arithmetic: 4.42 us -> 0.61 us
    reduce_scatter x2 -> x0, waiting for transfers between devices: 174 us -> none  [local(): lax.psum_scatter(partial_pred, 'vox', scatter_dimension=0, tiled=True)]
    pallas_call x0 -> x1, Pallas kernels: none -> 147 us  [local(): pl.pallas_call(functools.partial(kernel, A, B, NO, C, pred_scale, grad_sc...]
    all_gather x3 -> x0, waiting for transfers between devices: 126 us -> none  [the longest x2 102 us: local(): lax.all_gather(weighted_b, 'vox', axis=0, tiled=True)]
    dot_general x4 -> x0, matrix products: 19.2 us -> none  [the longest x2 10.8 us: local(): lax.dot_general(lax.all_gather(source_fields, 'opt', axis=0, tiled=True),...]
    psum x2 -> x0, blocking collectives: 12.3 us -> none  [local(): gradient = lax.psum(local_grad, 'opt') * grad_scale]
    convert_element_type x2 -> x0, other arithmetic: 3.82 us -> none  [local(): weighted_b = weighted.astype(jnp.bfloat16)]
  transfers between devices with their start and end apart: 5 -> 0, of which waited for: 5 -> 0; matrix products, arithmetic and copies ran while one was open for 0% -> 0% of each run, Pallas kernels for 0% -> 0%
where the time goes in v1:
time: 154 us; the launch traced here: 153 us
  Pallas kernels  147 us (95%)
  local copies, waits for them, and re-layouts  4.56 us (3%)
    pallas_call x1, Pallas kernels, local(): pl.pallas_call(functools.partial(kernel, A, B, NO, C, pred_scale, grad_sc...  147 us
    unnamed x7, local copies, waits for them, and re-layouts  3.87 us

profile of v1, /device:TPU:0, one launch (start us, length us, event | category | flops | bytes accessed | tf_op | source)
XLA Modules:
  0.0 152.8 jit_solution(7491441222436961290)
XLA Ops:
  0.6 0.7 reshape.14.mu_in
  1.3 0.0 copy-start
  1.3 1.0 copy-done
  2.4 0.0 copy-start.1
  2.4 1.0 copy-done.1
  3.4 0.0 copy-start.2
  3.4 1.0 copy-done.2
  4.4 147.0 %shard_map.77 = (f32[1,768]{1,0:T(1,128)S(1)}, f32[128,1024]{1,0:T(8,128)S(1)}) custom-call(bf16[2,128,768]{2,1,0:T(8,128)(2,1)S(1)} %bitcast.1, bf16[1024,768]{1,0:T(8,128)(2,1)} %d_ref.1, f32[128,1024]{1,0:T(8,128)S(1)} %copy-done, s32[128,1024]{1,0:T(8,128)S(1)} %copy-done.1, s32[128,1024]{1,0:T(8,128)} %class_ref.1, f32[1,768]{1,0:T(1,128)S(1)} %reshape.14.mu_in), custom_call_target="tpu_custom_call" | custom-call | tf_op jit(solution)/shard_map/pallas_call | solution.py:221
  151.4 0.6 reduce
  152.0 0.8 copy.9
Async XLA Ops:
  1.3 1.0 copy-start
  2.4 1.0 copy-start.1
  3.4 1.0 copy-start.2

commit v2 on v1

--- a/solution.py
+++ b/solution.py
@@ -14,11 +14,11 @@
 
 def kernel(
     A, B, NO, C, pred_scale, grad_scale,
-    s_ref, d_ref, meas_ref, valid_ref, class_ref, mu_in,
+    s_ref, d_in, meas_in, valid_in, class_in, mu_in,
     mu_ref, res_ref,
-    s_full, maskf, scaled, ysend, yrecv, own, zsend, zrecv, wfull, gbuf,
+    d_ref, meas_ref, valid_ref, class_ref, s_full, maskf, scaled, ysend, yrecv, own, zsend, zrecv, wfull, gbuf,
     sx_send, sx_recv, sc_send, sc_recv, y_send, y_recv, z_send, z_recv,
-    wz_send, wz_recv, wy_send, wy_recv, g_send, g_recv,
+    wz_send, wz_recv, wy_send, wy_recv, g_send, g_recv, in_sem,
 ):
     q, R, X = s_ref.shape
     W = d_ref.shape[0] // C
@@ -29,12 +29,26 @@
     NC = NO // 2
     mate = chip * 2 + 1 - core
     y_peers = [lax.rem(y + k, B) for k in range(1, B)]
+    up, down = z + 1, z - 1
     z_peers = [lax.rem(z + k, A) for k in range(1, A)]
     o_peers = [lax.rem(opt + k, NO) for k in range(1, NO)]
     c_peers = [lax.rem(chip + k, NC) for k in range(1, NC)]
 
+    def y_first(c):
+        return c % 2 == 1
+
     def at(zz, yy):
         return {"vox": zz * B + yy}
+
+    loads = [
+        pltpu.make_async_copy(valid_in, valid_ref, in_sem.at[0]),
+        pltpu.make_async_copy(class_in, class_ref, in_sem.at[1]),
+        pltpu.make_async_copy(s_ref, s_full.at[pl.ds(opt * q, q)], in_sem.at[2]),
+        pltpu.make_async_copy(d_in, d_ref, in_sem.at[3]),
+        pltpu.make_async_copy(meas_in, meas_ref, in_sem.at[4]),
+    ]
+    for load in loads:
+        load.start()
 
     barrier = pltpu.get_barrier_semaphore()
     for p in y_peers:
@@ -63,7 +77,8 @@
     for p in c_peers:
         to_chip(p, opt).start()
     to_mate(s_ref, opt).start()
-    s_full[pl.ds(opt * q, q)] = s_ref[...]
+    for load in loads:
+        load.wait()
     mu_ref[...] = mu_in[...]
     maskf[...] = valid_ref[...].astype(jnp.float32) / (1.0 + class_ref[...].astype(jnp.float32))
     for p in c_peers:
@@ -87,9 +102,24 @@
                 zsend.at[c, t], zrecv.at[it, c, src], z_send.at[c, t], z_recv.at[it, c, src], at(t, y)
             )
 
-        def wz_copy(c, t, src):
-            mine = wfull.at[it, c, src * B + y]
-            return remote(mine, mine, wz_send.at[c, t], wz_recv.at[it, c, src], at(t, y))
+        def wz_copy(c, src, yy, way):
+            mine = wfull.at[it, c, src * B + yy]
+            return remote(
+                mine, mine, wz_send.at[c, src, yy, way], wz_recv.at[it, c, src, yy],
+                at(up if way else down, y),
+            )
+
+        def can(way):
+            return z < A - 1 if way else z > 0
+
+        def spread(c, yy):
+            for way in (0, 1):
+                @pl.when(can(way))
+                def _():
+                    wz_copy(c, z, yy, way).start()
+
+        def columns(c):
+            return [y] + y_peers if y_first(c) else [y]
 
         def wy_copy(c, src, p, yy):
             mine = wfull.at[it, c, src * B + yy]
@@ -111,14 +141,21 @@
 
             for p in y_peers:
                 ysend[c, p] = part(p).astype(jnp.bfloat16)
+            if c == 0:
+                send_y(c)
+            own[c] = part(y)
+
+        def send_y(c):
+            for p in y_peers:
                 y_copy(c, p).start()
-            own[c] = part(y)
 
         def over_y(c):
             for p in y_peers:
                 remote(
                     ysend.at[c, p], yrecv.at[it, c, p], y_send.at[c, p], y_recv.at[it, c, p], at(z, p)
                 ).wait_recv()
+            if c + 1 < C:
+                send_y(c + 1)
             for t in z_peers:
                 total = own[c, t]
                 for p in y_peers:
@@ -139,19 +176,51 @@
             wfull[it, c, vox] = weighted.astype(jnp.bfloat16)
             for p in y_peers:
                 wy_copy(c, z, p, y).start()
+            spread(c, y)
+
+        def forward(c):
+            if y_first(c):
+                for p in y_peers:
+                    wy_copy(c, z, p, p).wait_recv()
+                    spread(c, p)
+            for k in range(1, A):
+                for way in (0, 1):
+                    src = z - k if way else z + k
+
+                    @pl.when(src >= 0 if way else src < A)
+                    def _():
+                        for yy in columns(c):
+                            wz_copy(c, src, yy, way).wait_recv()
+
+                            @pl.when(can(way))
+                            def _():
+                                wz_copy(c, src, yy, way).start()
+
+                        if not y_first(c):
+                            for p in y_peers:
+                                wy_copy(c, src, p, y).start()
+
+        def sent(c):
+            for p in y_peers:
+                y_copy(c, p).wait_send()
+                for src in [z] if y_first(c) else range(A):
+                    wy_copy(c, src, p, y).wait_send()
             for t in z_peers:
-                wz_copy(c, t, z).start()
-
-        def forward(c):
-            for t in z_peers:
-                wz_copy(c, t, t).wait_recv()
-                for p in y_peers:
-                    wy_copy(c, t, p, y).start()
+                z_copy(c, t, z).wait_send()
+            for k in range(A):
+                for way in (0, 1):
+                    src = z - k if way else z + k
+
+                    @pl.when(jnp.logical_and(src >= 0 if way else src < A, can(way)))
+                    def _():
+                        for yy in columns(c):
+                            wz_copy(c, src, yy, way).wait_send()
 
         def gradient(c, total):
-            for t in range(A):
-                for p in y_peers:
-                    wy_copy(c, t, p, p).wait_recv()
+            if not y_first(c):
+                for t in range(A):
+                    for p in y_peers:
+                        wy_copy(c, t, p, p).wait_recv()
             d = d_ref[pl.ds(c * W, W)]
 
             def rows(a, total):
@@ -162,12 +231,15 @@
 
             return lax.fori_loop(0, A, rows, total)
 
-        for c in range(C):
-            predict(c)
+        predict(0)
+        if C > 1:
+            predict(1)
         total = jnp.zeros((8, X), jnp.float32)
         for slot in range(C + 4):
             if slot < C:
                 over_y(slot)
+            if slot + 2 < C:
+                predict(slot + 2)
             if 0 <= slot - 1 < C:
                 over_z(slot - 1)
             if 0 <= slot - 2 < C:
@@ -183,13 +255,7 @@
         for p in o_peers:
             g_copy(p, opt).start()
         for c in range(C):
-            for p in y_peers:
-                y_copy(c, p).wait_send()
-                for t in range(A):
-                    wy_copy(c, t, p, y).wait_send()
-            for t in z_peers:
-                z_copy(c, t, z).wait_send()
-                wz_copy(c, t, z).wait_send()
+            sent(c)
         for p in o_peers:
             g_copy(p, p).wait_recv()
         total = gbuf[it, 0]
@@ -224,9 +290,13 @@
             jax.ShapeDtypeStruct((1, X), f32),
             jax.ShapeDtypeStruct((R, DL), f32),
         ),
-        in_specs=[vmem] * 6,
+        in_specs=[pl.BlockSpec(memory_space=pl.ANY)] * 5 + [vmem],
         out_specs=(vmem, vmem),
         scratch_shapes=[
+            pltpu.VMEM((DL, X), bf),
+            pltpu.VMEM((R, DL), f32),
+            pltpu.VMEM((R, DL), jnp.int32),
+            pltpu.VMEM((R, DL), jnp.int32),
             pltpu.VMEM((A * B, R, X), bf),
             pltpu.VMEM((R, DL), f32),
             pltpu.VMEM((W, X), bf),
@@ -240,9 +310,10 @@
             dma((NO // 2,)), dma((NO,)), dma((NO,)), dma((NO,)),
             dma((C, B)), dma((ITERS, C, B)),
             dma((C, A)), dma((ITERS, C, A)),
-            dma((C, A)), dma((ITERS, C, A)),
+            dma((C, A, B, 2)), dma((ITERS, C, A, B)),
             dma((C, A, B)), dma((ITERS, C, A, B)),
             dma((NO,)), dma((ITERS, NO)),
+            dma((5,)),
         ],
         compiler_params=pltpu.CompilerParams(
             collective_id=0, has_side_effects=True, vmem_limit_bytes=52 * 1024 * 1024

time: 154 us -> 166 us (1.078)
  Pallas kernels: 147 us -> 159 us
    pallas_call x1, Pallas kernels: 147 us -> 159 us  [local(): pl.pallas_call(functools.partial(kernel, A, B, NO, C, pred_scale, grad_sc...]
where the time goes in v2:
time: 166 us; the launch traced here: 165 us
  Pallas kernels  159 us (96%)
  local copies, waits for them, and re-layouts  4.56 us (3%)
    pallas_call x1, Pallas kernels, local(): pl.pallas_call(functools.partial(kernel, A, B, NO, C, pred_scale, grad_sc...  159 us
    unnamed x7, local copies, waits for them, and re-layouts  3.87 us

profile of v2, /device:TPU:0, one launch (start us, length us, event | category | flops | bytes accessed | tf_op | source)
XLA Modules:
  0.0 165.3 jit_solution(8707758206922443485)
XLA Ops:
  0.6 0.7 reshape.14.mu_in
  1.3 0.0 copy-start
  1.3 1.0 copy-done
  2.4 0.0 copy-start.1
  2.4 1.0 copy-done.1
  3.4 0.0 copy-start.2
  3.4 1.0 copy-done.2
  4.4 159.5 %shard_map.77 = (f32[1,768]{1,0:T(1,128)S(1)}, f32[128,1024]{1,0:T(8,128)S(1)}) custom-call(bf16[2,128,768]{2,1,0:T(8,128)(2,1)S(1)} %bitcast.1, bf16[1024,768]{1,0:T(8,128)(2,1)} %d_in.1, f32[128,1024]{1,0:T(8,128)S(1)} %copy-done, s32[128,1024]{1,0:T(8,128)S(1)} %copy-done.1, s32[128,1024]{1,0:T(8,128)} %class_in.1, f32[1,768]{1,0:T(1,128)S(1)} %reshape.14.mu_in), custom_call_target="tpu_custom_call" | custom-call | tf_op jit(solution)/shard_map/pallas_call | solution.py:287
  163.9 0.6 reduce
  164.5 0.8 copy.9
Async XLA Ops:
  1.3 1.0 copy-start
  2.4 1.0 copy-start.1
  3.4 1.0 copy-start.2

commit v3 on v0

v3 whole, which is shorter than its diff:
```python
import functools

import jax
import jax.numpy as jnp
import numpy as np
from jax import lax
from jax.experimental import pallas as pl
from jax.experimental.pallas import tpu as pltpu
from jax.sharding import PartitionSpec as P

ITERS = 2
MESH = pl.DeviceIdType.MESH


def kernel(
    A, B, NO, W, pred_scale, grad_scale,
    s_in, d_in, meas_in, valid_in, class_in, mu_in,
    mu_out, res_ref,
    s_full, d_full, meas_ref, valid_ref, class_ref, codes, code_ref, mu_ref, scaled,
    own, zsend, zrecv, wfull, rsend, rrecv, gbuf,
    sy_send, sy_recv, sx_send, sx_recv, sm_send, sm_recv, d_send, d_recv,
    p_send, p_recv, r_send, r_recv, z_send, z_recv, w_send, w_recv, g_send, g_recv, in_sem,
):
    q, R, X = s_in.shape
    H = d_in.shape[0] // B
    NH = H // W
    C = NH * B
    vox = lax.axis_index("vox")
    opt = lax.axis_index("opt")
    z, y = vox // B, lax.rem(vox, B)
    chip, core = opt // 2, lax.rem(opt, 2)
    NC = NO // 2
    mate = chip * 2 + 1 - core
    rows_y = [lax.rem(y + k, B) for k in range(B)]
    y_peers = rows_y[1:]
    z_peers = [lax.rem(z + k, A) for k in range(1, A)]
    c_peers = [lax.rem(chip + k, NC) for k in range(1, NC)]
    group = [
        (lax.rem(y + k, B), lax.rem(opt + j, NO)) for k in range(B) for j in range(NO) if k + j > 0
    ]

    def remote(src, dst, send, recv, where):
        return pltpu.make_async_remote_copy(
            src_ref=src, dst_ref=dst, send_sem=send, recv_sem=recv,
            device_id=where, device_id_type=MESH,
        )

    def half(yy):
        return pl.ds(pl.multiple_of(yy * X, X), X)

    def cols(yy):
        return pl.ds(pl.multiple_of(yy * H, H), H)

    def at_y(p):
        return {"vox": z * B + p}

    def at_z(t):
        return {"vox": t * B + y}

    def block(j, yy):
        return s_full.at[pl.ds(j * q, q), :, half(yy)]

    def d_block(h, yy):
        return d_full.at[pl.ds(h * W, W), half(yy)]

    def d_rows(h, yy):
        return d_in.at[pl.ds(pl.multiple_of(yy * H + h * W, W), W)]

    loads = [
        pltpu.make_async_copy(valid_in, valid_ref, in_sem.at[0]),
        pltpu.make_async_copy(class_in, class_ref, in_sem.at[1]),
        pltpu.make_async_copy(s_in, block(opt, y), in_sem.at[2]),
        pltpu.make_async_copy(meas_in.at[:, cols(y)], meas_ref.at[y], in_sem.at[3]),
    ] + [
        pltpu.make_async_copy(d_rows(h, y), d_block(h, y), in_sem.at[4 + h]) for h in range(NH)
    ]
    for load in loads:
        load.start()

    barrier = pltpu.get_barrier_semaphore()
    for t in z_peers:
        pl.semaphore_signal(barrier, inc=1, device_id=at_z(t), device_id_type=MESH)
    for p, j in group:
        pl.semaphore_signal(
            barrier, inc=1, device_id={"vox": z * B + p, "opt": j}, device_id_type=MESH
        )
    pl.semaphore_wait(barrier, A - 1 + B * NO - 1)

    def s_y(p, yy):
        return remote(s_in, block(opt, yy), sy_send.at[p], sy_recv.at[yy], at_y(p))

    def s_x(p, j, yy):
        return remote(
            block(j, yy), block(j, yy), sx_send.at[p, yy], sx_recv.at[j // 2, yy],
            {"opt": p * 2 + core},
        )

    def s_x_own(p):
        return remote(
            s_in, block(opt, y), sx_send.at[p, y], sx_recv.at[chip, y], {"opt": p * 2 + core}
        )

    def s_m(p, cc, yy):
        mine = block(p * 2 + cc, yy)
        return remote(mine, mine, sm_send.at[p, yy], sm_recv.at[p, yy], {"opt": mate})

    def s_m_own():
        return remote(s_in, block(opt, y), sm_send.at[chip, y], sm_recv.at[chip, y], {"opt": mate})

    def d_y(h, p, yy):
        return remote(d_rows(h, p), d_block(h, yy), d_send.at[h, p], d_recv.at[h, yy], at_y(p))

    def pairs(p, yy):
        return [
            remote(mu_in, mu_ref.at[:, half(yy)], p_send.at[0, p], p_recv.at[0, yy], at_y(p)),
            remote(
                meas_in.at[:, cols(p)], meas_ref.at[yy], p_send.at[1, p], p_recv.at[1, yy], at_y(p)
            ),
            remote(
                codes.at[:, cols(p)], code_ref.at[yy], p_send.at[2, p], p_recv.at[2, yy], at_y(p)
            ),
        ]

    for p in y_peers:
        s_y(p, y).start()
    for p in c_peers:
        s_x_own(p).start()
    s_m_own().start()
    for p in y_peers:
        pairs(p, y)[0].start()
    for load in loads:
        load.wait()
    mu_ref[:, half(y)] = mu_in[...]
    codes[...] = (valid_ref[...] * (1 + class_ref[...])).astype(jnp.float32).astype(jnp.bfloat16)
    code_ref[y] = codes[:, cols(y)]
    for p in y_peers:
        s_y(p, p).wait_recv()
        d_y(0, p, y).start()
        for pp in c_peers:
            s_x(pp, opt, p).start()
        s_m(chip, core, p).start()
    for yy in rows_y:
        for p in c_peers:
            s_x(p, p * 2 + core, yy).wait_recv()
            s_m(p, core, yy).start()
    for p in y_peers:
        for copy in pairs(p, y)[1:]:
            copy.start()
        for h in range(1, NH):
            d_y(h, p, y).start()
    for yy in rows_y:
        for p in range(NC):
            s_m(p, 1 - core, yy).wait_recv()
    for p in y_peers:
        pairs(p, p)[0].wait_recv()
        s_y(p, y).wait_send()
    for p in c_peers:
        s_x_own(p).wait_send()
        for yy in y_peers:
            s_x(p, opt, yy).wait_send()
    for p in range(NC):
        for yy in rows_y:
            s_m(p, core, yy).wait_send()

    def back(h, p, yy):
        return remote(
            rsend.at[h, p], rrecv.at[h, yy], r_send.at[h, p], r_recv.at[h, yy], at_y(p)
        )

    def step(it, carry):
        def z_copy(c, t, src):
            return remote(
                zsend.at[c, t], zrecv.at[it, c, src], z_send.at[c, t], z_recv.at[it, c, src], at_z(t)
            )

        def w_copy(c, t, src):
            mine = wfull.at[it, c, src]
            return remote(mine, mine, w_send.at[c, t], w_recv.at[it, c, src], at_z(t))

        def predict(c):
            h, r = c // B, rows_y[c % B]
            if c % B == 0:
                @pl.when(it == 0)
                def _():
                    for p in y_peers:
                        d_y(h, p, p).wait_recv()

                scaled[...] = (
                    d_full[pl.ds(h * W, W)].astype(jnp.float32) * mu_ref[...]
                ).astype(jnp.bfloat16)
            rows = jnp.concatenate([s_full[a * B + r] for a in range(A)], axis=0)
            part = lax.dot_general(
                rows, scaled[...], (((1,), (1,)), ((), ())), preferred_element_type=jnp.float32
            ).reshape(A, R, W)
            zsend[c] = part.astype(jnp.bfloat16)
            for t in z_peers:
                z_copy(c, t, z).start()
            own[c] = part

        def over_z(c):
            h, k = c // B, c % B
            r = rows_y[k]
            if h == 0 and k > 0:
                @pl.when(it == 0)
                def _():
                    for copy in pairs(r, r)[1:]:
                        copy.wait_recv()

            total = own[c, z]
            for t in z_peers:
                z_copy(c, t, t).wait_recv()
                total = total + zrecv[it, c, t].astype(jnp.float32)
            here = pl.ds(h * W, W)
            code = code_ref[r, :, here].astype(jnp.float32)
            weight = jnp.where(code > 0.0, 1.0 / jnp.maximum(code, 1.0), 0.0)
            weighted = weight * (total * pred_scale - meas_ref[r, :, here])
            wfull[it, c, z] = weighted.astype(jnp.bfloat16)
            for t in z_peers:
                w_copy(c, t, z).start()
            rsend[h, r] = weighted
            if k > 0:
                @pl.when(it == ITERS - 1)
                def _():
                    back(h, r, y).start()

        def gradient(c, total):
            h, r = c // B, rows_y[c % B]
            for t in z_peers:
                w_copy(c, t, t).wait_recv()
            d = d_full[pl.ds(h * W, W)]

            def rows(i, total):
                w = wfull[it, c, pl.ds(2 * i, 2)].reshape(2 * R, W)
                s = jnp.concatenate([s_full[(2 * i + k) * B + r] for k in range(2)], axis=0)
                inner = jnp.dot(w, d, preferred_element_type=jnp.float32) * s.astype(jnp.float32)
                return total + jnp.sum(inner.reshape(2 * R // 8, 8, B * X), axis=0)

            return lax.fori_loop(0, A // 2, rows, total)

        total = jnp.zeros((8, B * X), jnp.float32)
        for c in range(min(2, C)):
            predict(c)
        for slot in range(C + 1):
            if slot + 2 < C:
                predict(slot + 2)
            if slot < C:
                over_z(slot)
            if slot > 0:
                total = gradient(slot - 1, total)

        def g_copy(p, j, sp, sj):
            mine = gbuf.at[it, sp * NO + sj]
            return remote(
                mine, mine, g_send.at[p * NO + j], g_recv.at[it, sp * NO + sj],
                {"vox": z * B + p, "opt": j},
            )

        gbuf[it, y * NO + opt] = jnp.sum(total, axis=0, keepdims=True)
        for p, j in group:
            g_copy(p, j, y, opt).start()
        for c in range(C):
            for t in z_peers:
                z_copy(c, t, z).wait_send()
                w_copy(c, t, z).wait_send()
        for p, j in group:
            g_copy(p, j, p, j).wait_recv()
        grad = gbuf[it, 0]
        for j in range(1, B * NO):
            grad = grad + gbuf[it, j]
        mu_ref[...] = jnp.maximum(mu_ref[...] - 2.0 * (grad * grad_scale), 0.0)
        for p, j in group:
            g_copy(p, j, y, opt).wait_send()
        return carry

    lax.fori_loop(0, ITERS, step, 0)
    mu_out[...] = mu_ref[:, half(y)]
    for h in range(NH):
        res_ref[:, pl.ds(pl.multiple_of(y * H + h * W, W), W)] = rsend[h, y]
        for p in y_peers:
            back(h, p, p).wait_recv()
            res_ref[:, pl.ds(pl.multiple_of(p * H + h * W, W), W)] = rrecv[h, p]
            back(h, p, y).wait_send()
            d_y(h, p, y).wait_send()
    for p in y_peers:
        for copy in pairs(p, y):
            copy.wait_send()


def local(source_fields, detector_fields, measured, valid_pair, weight_class, absorption):
    NV, NO = lax.axis_size("vox"), lax.axis_size("opt")
    R, DL = measured.shape
    X = absorption.shape[0]
    q = source_fields.shape[0] // R
    B = 2 if DL % 256 == 0 and NV % 4 == 0 else 1
    A = NV // B
    H = DL // B
    W = min(H, 256)
    NH = H // W
    C = NH * B
    pred_scale = float(np.float32(1.0) / np.sqrt(np.float32(X * NV)))
    grad_scale = float(np.sqrt(np.float32(X * NV)) / np.float32(R * NV * DL * NO))
    bf, f32 = jnp.bfloat16, jnp.float32
    dma = pltpu.SemaphoreType.DMA
    vmem = pl.BlockSpec(memory_space=pltpu.VMEM)
    mu, weighted = pl.pallas_call(
        functools.partial(kernel, A, B, NO, W, pred_scale, grad_scale),
        out_shape=(
            jax.ShapeDtypeStruct((1, X), f32),
            jax.ShapeDtypeStruct((R, DL), f32),
        ),
        in_specs=[pl.BlockSpec(memory_space=pl.ANY)] * 5 + [vmem],
        out_specs=(vmem, vmem),
        scratch_shapes=[
            pltpu.VMEM((A * B, R, B * X), bf),
            pltpu.VMEM((H, B * X), bf),
            pltpu.VMEM((B, R, H), f32),
            pltpu.VMEM((R, DL), jnp.int32),
            pltpu.VMEM((R, DL), jnp.int32),
            pltpu.VMEM((R, DL), bf),
            pltpu.VMEM((B, R, H), bf),
            pltpu.VMEM((1, B * X), f32),
            pltpu.VMEM((W, B * X), bf),
            pltpu.VMEM((C, A, R, W), f32),
            pltpu.VMEM((C, A, R, W), bf),
            pltpu.VMEM((ITERS, C, A, R, W), bf),
            pltpu.VMEM((ITERS, C, A, R, W), bf),
            pltpu.VMEM((NH, B, R, W), f32),
            pltpu.VMEM((NH, B, R, W), f32),
            pltpu.VMEM((ITERS, B * NO, 1, B * X), f32),
            dma((B,)), dma((B,)),
            dma((NO // 2, B)), dma((NO // 2, B)),
            dma((NO // 2, B)), dma((NO // 2, B)),
            dma((NH, B)), dma((NH, B)),
            dma((3, B)), dma((3, B)),
            dma((NH, B)), dma((NH, B)),
            dma((C, A)), dma((ITERS, C, A)),
            dma((C, A)), dma((ITERS, C, A)),
            dma((B * NO,)), dma((ITERS, B * NO)),
            dma((4 + NH,)),
        ],
        compiler_params=pltpu.CompilerParams(
            collective_id=0, has_side_effects=True, vmem_limit_bytes=52 * 1024 * 1024
        ),
    )(
        source_fields.reshape(q, R, X), detector_fields, measured, valid_pair, weight_class,
        absorption.reshape(1, X),
    )
    return mu.reshape(X), weighted


def solution(mesh):
    placed = (
        P("opt", "vox"),
        P("opt", "vox"),
        P("vox", "opt"),
        P("vox", "opt"),
        P("vox", "opt"),
        P("vox"),
    )
    return jax.shard_map(
        local, mesh=mesh, in_specs=placed, out_specs=(P("vox"), P("vox", "opt")), check_vma=False
    )
```

time: 353 us -> 142 us (0.40)
  waiting for transfers between devices: 300 us -> 0 us
  Pallas kernels: 0 us -> 136 us
  matrix products: 19.2 us -> 0 us
  between operations: 13.9 us -> 0.64 us
  blocking collectives: 12.3 us -> 0 us
  other arithmetic: 4.42 us -> 0.61 us
    reduce_scatter x2 -> x0, waiting for transfers between devices: 174 us -> none  [local(): lax.psum_scatter(partial_pred, 'vox', scatter_dimension=0, tiled=True)]
    pallas_call x0 -> x1, Pallas kernels: none -> 136 us  [local(): pl.pallas_call(functools.partial(kernel, A, B, NO, W, pred_scale, grad_sc...]
    all_gather x3 -> x0, waiting for transfers between devices: 126 us -> none  [the longest x2 102 us: local(): lax.all_gather(weighted_b, 'vox', axis=0, tiled=True)]
    dot_general x4 -> x0, matrix products: 19.2 us -> none  [the longest x2 10.8 us: local(): lax.dot_general(lax.all_gather(source_fields, 'opt', axis=0, tiled=True),...]
    psum x2 -> x0, blocking collectives: 12.3 us -> none  [local(): gradient = lax.psum(local_grad, 'opt') * grad_scale]
    convert_element_type x2 -> x0, other arithmetic: 3.82 us -> none  [local(): weighted_b = weighted.astype(jnp.bfloat16)]
  transfers between devices with their start and end apart: 5 -> 0, of which waited for: 5 -> 0; matrix products, arithmetic and copies ran while one was open for 0% -> 0% of each run, Pallas kernels for 0% -> 0%
where the time goes in v3:
time: 142 us
  Pallas kernels  136 us (96%)
  local copies, waits for them, and re-layouts  4.56 us (3%)
    pallas_call x1, Pallas kernels, local(): pl.pallas_call(functools.partial(kernel, A, B, NO, W, pred_scale, grad_sc...  136 us
    unnamed x7, local copies, waits for them, and re-layouts  3.87 us

profile of v3, /device:TPU:0, one launch (start us, length us, event | category | flops | bytes accessed | tf_op | source)
XLA Modules:
  0.0 142.0 jit_solution(3711214003337620176)
XLA Ops:
  0.6 0.7 reshape.14.mu_in
  1.3 0.0 copy-start
  1.3 1.0 copy-done
  2.4 0.0 copy-start.1
  2.4 1.0 copy-done.1
  3.4 0.0 copy-start.2
  3.4 1.0 copy-done.2
  4.4 136.2 %shard_map.77 = (f32[1,768]{1,0:T(1,128)S(1)}, f32[128,1024]{1,0:T(8,128)S(1)}) custom-call(bf16[2,128,768]{2,1,0:T(8,128)(2,1)S(1)} %bitcast.1, bf16[1024,768]{1,0:T(8,128)(2,1)} %d_in.1, f32[128,1024]{1,0:T(8,128)S(1)} %copy-done, s32[128,1024]{1,0:T(8,128)S(1)} %copy-done.1, s32[128,1024]{1,0:T(8,128)} %class_in.1, f32[1,768]{1,0:T(1,128)S(1)} %reshape.14.mu_in), custom_call_target="tpu_custom_call" | custom-call | tf_op jit(solution)/shard_map/pallas_call | solution.py:305
  140.6 0.6 reduce
  141.2 0.8 copy.9
Async XLA Ops:
  1.3 1.0 copy-start
  2.4 1.0 copy-start.1
  3.4 1.0 copy-start.2

commit v4 on v3

--- a/solution.py
+++ b/solution.py
@@ -17,9 +17,9 @@
     s_in, d_in, meas_in, valid_in, class_in, mu_in,
     mu_out, res_ref,
     s_full, d_full, meas_ref, valid_ref, class_ref, codes, code_ref, mu_ref, scaled,
-    own, zsend, zrecv, wfull, rsend, rrecv, gbuf,
+    own, zsend, zrecv, zrel, wfull, rsend, rrecv, gbuf,
     sy_send, sy_recv, sx_send, sx_recv, sm_send, sm_recv, d_send, d_recv,
-    p_send, p_recv, r_send, r_recv, z_send, z_recv, w_send, w_recv, g_send, g_recv, in_sem,
+    p_send, p_recv, r_send, r_recv, z_send, z_recv, rel_recv, w_send, w_recv, g_send, g_recv, in_sem,
 ):
     q, R, X = s_in.shape
     H = d_in.shape[0] // B
@@ -34,6 +34,10 @@
     rows_y = [lax.rem(y + k, B) for k in range(B)]
     y_peers = rows_y[1:]
     z_peers = [lax.rem(z + k, A) for k in range(1, A)]
+    line = A == 4
+    inner = lax.rem((z + 1) // 2, 2)
+    near = inner * 3 * (z - 1) + (1 - inner) * (1 + z // 3)
+    far = inner * 3 * (2 - z) + (1 - inner) * (3 - z)
     c_peers = [lax.rem(chip + k, NC) for k in range(1, NC)]
     group = [
         (lax.rem(y + k, B), lax.rem(opt + j, NO)) for k in range(B) for j in range(NO) if k + j > 0
@@ -173,6 +177,21 @@
                 zsend.at[c, t], zrecv.at[it, c, src], z_send.at[c, t], z_recv.at[it, c, src], at_z(t)
             )
 
+        def rel_copy(c):
+            return remote(
+                zsend.at[c, far], zrel.at[it, c], z_send.at[c, far], rel_recv.at[it, c], at_z(near)
+            )
+
+        def hand_on(c):
+            mine = wfull.at[it, c, far]
+            return remote(mine, mine, w_send.at[c, z], w_recv.at[it, c, far], at_z(near))
+
+        def where(cond, run):
+            if line:
+                pl.when(cond)(run)
+            else:
+                run()
+
         def w_copy(c, t, src):
             mine = wfull.at[it, c, src]
             return remote(mine, mine, w_send.at[c, t], w_recv.at[it, c, src], at_z(t))
@@ -194,8 +213,27 @@
             ).reshape(A, R, W)
             zsend[c] = part.astype(jnp.bfloat16)
             for t in z_peers:
-                z_copy(c, t, z).start()
+                where(t != far, lambda: z_copy(c, t, z).start())
+            if line:
+                @pl.when(inner == 0)
+                def _():
+                    rel_copy(c).start()
             own[c] = part
+
+        def relay(c):
+            if line:
+                @pl.when(inner == 1)
+                def _():
+                    rel_copy(c).wait_recv()
+                    zsend[c, far] = (own[c, far] + zrel[it, c].astype(jnp.float32)).astype(jnp.bfloat16)
+                    z_copy(c, far, z).start()
+
+        def forward(c):
+            if line:
+                @pl.when(inner == 1)
+                def _():
+                    w_copy(c, far, far).wait_recv()
+                    hand_on(c).start()
 
         def over_z(c):
             h, k = c // B, c % B
@@ -206,17 +244,20 @@
                     for copy in pairs(r, r)[1:]:
                         copy.wait_recv()
 
+            for t in z_peers:
+                def add():
+                    z_copy(c, t, t).wait_recv()
+                    own[c, z] = own[c, z] + zrecv[it, c, t].astype(jnp.float32)
+
+                where(jnp.logical_or(inner == 1, t != far), add)
             total = own[c, z]
-            for t in z_peers:
-                z_copy(c, t, t).wait_recv()
-                total = total + zrecv[it, c, t].astype(jnp.float32)
             here = pl.ds(h * W, W)
             code = code_ref[r, :, here].astype(jnp.float32)
             weight = jnp.where(code > 0.0, 1.0 / jnp.maximum(code, 1.0), 0.0)
             weighted = weight * (total * pred_scale - meas_ref[r, :, here])
             wfull[it, c, z] = weighted.astype(jnp.bfloat16)
             for t in z_peers:
-                w_copy(c, t, z).start()
+                where(jnp.logical_or(inner == 1, t != far), lambda: w_copy(c, t, z).start())
             rsend[h, r] = weighted
             if k > 0:
                 @pl.when(it == ITERS - 1)
@@ -226,7 +267,7 @@
         def gradient(c, total):
             h, r = c // B, rows_y[c % B]
             for t in z_peers:
-                w_copy(c, t, t).wait_recv()
+                where(jnp.logical_or(inner == 0, t != far), lambda: w_copy(c, t, t).wait_recv())
             d = d_full[pl.ds(h * W, W)]
 
             def rows(i, total):
@@ -240,13 +281,18 @@
         total = jnp.zeros((8, B * X), jnp.float32)
         for c in range(min(2, C)):
             predict(c)
-        for slot in range(C + 1):
+        relay(0)
+        for slot in range(C + 2):
             if slot + 2 < C:
                 predict(slot + 2)
+            if slot + 1 < C:
+                relay(slot + 1)
+            if 0 < slot <= C:
+                forward(slot - 1)
             if slot < C:
                 over_z(slot)
-            if slot > 0:
-                total = gradient(slot - 1, total)
+            if slot > 1:
+                total = gradient(slot - 2, total)
 
         def g_copy(p, j, sp, sj):
             mine = gbuf.at[it, sp * NO + sj]
@@ -261,7 +307,11 @@
         for c in range(C):
             for t in z_peers:
                 z_copy(c, t, z).wait_send()
-                w_copy(c, t, z).wait_send()
+                where(jnp.logical_or(inner == 1, t != far), lambda: w_copy(c, t, z).wait_send())
+            if line:
+                @pl.when(inner == 1)
+                def _():
+                    hand_on(c).wait_send()
         for p, j in group:
             g_copy(p, j, p, j).wait_recv()
         grad = gbuf[it, 0]
@@ -323,6 +373,7 @@
             pltpu.VMEM((C, A, R, W), f32),
             pltpu.VMEM((C, A, R, W), bf),
             pltpu.VMEM((ITERS, C, A, R, W), bf),
+            pltpu.VMEM((ITERS, C, R, W), bf),
             pltpu.VMEM((ITERS, C, A, R, W), bf),
             pltpu.VMEM((NH, B, R, W), f32),
             pltpu.VMEM((NH, B, R, W), f32),
@@ -333,7 +384,7 @@
             dma((NH, B)), dma((NH, B)),
             dma((3, B)), dma((3, B)),
             dma((NH, B)), dma((NH, B)),
-            dma((C, A)), dma((ITERS, C, A)),
+            dma((C, A)), dma((ITERS, C, A)), dma((ITERS, C)),
             dma((C, A)), dma((ITERS, C, A)),
             dma((B * NO,)), dma((ITERS, B * NO)),
             dma((4 + NH,)),

time: 142 us -> 128 us (0.901)
  Pallas kernels: 136 us -> 122 us
    pallas_call x1, Pallas kernels: 136 us -> 122 us  [local(): pl.pallas_call(functools.partial(kernel, A, B, NO, W, pred_scale, grad_sc...]
where the time goes in v4:
time: 128 us
  Pallas kernels  122 us (95%)
  local copies, waits for them, and re-layouts  4.56 us (4%)
    pallas_call x1, Pallas kernels, local(): pl.pallas_call(functools.partial(kernel, A, B, NO, W, pred_scale, grad_sc...  122 us
    unnamed x7, local copies, waits for them, and re-layouts  3.87 us

profile of v4, /device:TPU:0, one launch (start us, length us, event | category | flops | bytes accessed | tf_op | source)
XLA Modules:
  0.0 127.9 jit_solution(12116465106251471583)
XLA Ops:
  0.6 0.7 reshape.14.mu_in
  1.3 0.0 copy-start
  1.3 1.0 copy-done
  2.4 0.0 copy-start.1
  2.4 1.0 copy-done.1
  3.4 0.0 copy-start.2
  3.4 1.0 copy-done.2
  4.4 122.1 %shard_map.77 = (f32[1,768]{1,0:T(1,128)S(1)}, f32[128,1024]{1,0:T(8,128)S(1)}) custom-call(bf16[2,128,768]{2,1,0:T(8,128)(2,1)S(1)} %bitcast.1, bf16[1024,768]{1,0:T(8,128)(2,1)} %d_in.1, f32[128,1024]{1,0:T(8,128)S(1)} %copy-done, s32[128,1024]{1,0:T(8,128)S(1)} %copy-done.1, s32[128,1024]{1,0:T(8,128)} %class_in.1, f32[1,768]{1,0:T(1,128)S(1)} %reshape.14.mu_in), custom_call_target="tpu_custom_call" | custom-call | tf_op jit(solution)/shard_map/pallas_call | solution.py:355
  126.5 0.6 reduce
  127.1 0.8 copy.9
Async XLA Ops:
  1.3 1.0 copy-start
  2.4 1.0 copy-start.1
  3.4 1.0 copy-start.2

commit v5 on v4

--- a/solution.py
+++ b/solution.py
@@ -19,7 +19,7 @@
     s_full, d_full, meas_ref, valid_ref, class_ref, codes, code_ref, mu_ref, scaled,
     own, zsend, zrecv, zrel, wfull, rsend, rrecv, gbuf,
     sy_send, sy_recv, sx_send, sx_recv, sm_send, sm_recv, d_send, d_recv,
-    p_send, p_recv, r_send, r_recv, z_send, z_recv, rel_recv, w_send, w_recv, g_send, g_recv, in_sem,
+    p_send, p_recv, r_send, r_recv, z_send, z_recv, rel_send, rel_recv, h_send, w_send, w_recv, g_send, g_recv, in_sem,
 ):
     q, R, X = s_in.shape
     H = d_in.shape[0] // B
@@ -37,7 +37,10 @@
     line = A == 4
     inner = lax.rem((z + 1) // 2, 2)
     near = inner * 3 * (z - 1) + (1 - inner) * (1 + z // 3)
-    far = inner * 3 * (2 - z) + (1 - inner) * (3 - z)
+    across = 2 - z // 2
+    base = 2 * (1 - z // 2)
+    z_direct = [near] if line else z_peers
+    z_adds = [near, across] if line else z_peers
     c_peers = [lax.rem(chip + k, NC) for k in range(1, NC)]
     group = [
         (lax.rem(y + k, B), lax.rem(opt + j, NO)) for k in range(B) for j in range(NO) if k + j > 0
@@ -179,18 +182,13 @@
 
         def rel_copy(c):
             return remote(
-                zsend.at[c, far], zrel.at[it, c], z_send.at[c, far], rel_recv.at[it, c], at_z(near)
+                zsend.at[c, pl.ds(base, 2)], zrel.at[it, c], rel_send.at[c], rel_recv.at[it, c],
+                at_z(near),
             )
 
-        def hand_on(c):
-            mine = wfull.at[it, c, far]
-            return remote(mine, mine, w_send.at[c, z], w_recv.at[it, c, far], at_z(near))
-
-        def where(cond, run):
-            if line:
-                pl.when(cond)(run)
-            else:
-                run()
+        def hand_on(c, src):
+            mine = wfull.at[it, c, src]
+            return remote(mine, mine, h_send.at[c, src], w_recv.at[it, c, src], at_z(near))
 
         def w_copy(c, t, src):
             mine = wfull.at[it, c, src]
@@ -212,8 +210,8 @@
                 rows, scaled[...], (((1,), (1,)), ((), ())), preferred_element_type=jnp.float32
             ).reshape(A, R, W)
             zsend[c] = part.astype(jnp.bfloat16)
-            for t in z_peers:
-                where(t != far, lambda: z_copy(c, t, z).start())
+            for t in z_direct:
+                z_copy(c, t, z).start()
             if line:
                 @pl.when(inner == 0)
                 def _():
@@ -225,15 +223,19 @@
                 @pl.when(inner == 1)
                 def _():
                     rel_copy(c).wait_recv()
-                    zsend[c, far] = (own[c, far] + zrel[it, c].astype(jnp.float32)).astype(jnp.bfloat16)
-                    z_copy(c, far, z).start()
+                    both = pl.ds(base, 2)
+                    total = own[c, both] + zrel[it, c].astype(jnp.float32)
+                    zsend[c, both] = total.astype(jnp.bfloat16)
+                    for k in range(2):
+                        z_copy(c, base + k, z).start()
 
         def forward(c):
             if line:
                 @pl.when(inner == 1)
                 def _():
-                    w_copy(c, far, far).wait_recv()
-                    hand_on(c).start()
+                    for k in range(2):
+                        w_copy(c, base + k, base + k).wait_recv()
+                        hand_on(c, base + k).start()
 
         def over_z(c):
             h, k = c // B, c % B
@@ -244,20 +246,17 @@
                     for copy in pairs(r, r)[1:]:
                         copy.wait_recv()
 
-            for t in z_peers:
-                def add():
-                    z_copy(c, t, t).wait_recv()
-                    own[c, z] = own[c, z] + zrecv[it, c, t].astype(jnp.float32)
-
-                where(jnp.logical_or(inner == 1, t != far), add)
             total = own[c, z]
+            for t in z_adds:
+                z_copy(c, t, t).wait_recv()
+                total = total + zrecv[it, c, t].astype(jnp.float32)
             here = pl.ds(h * W, W)
             code = code_ref[r, :, here].astype(jnp.float32)
             weight = jnp.where(code > 0.0, 1.0 / jnp.maximum(code, 1.0), 0.0)
             weighted = weight * (total * pred_scale - meas_ref[r, :, here])
             wfull[it, c, z] = weighted.astype(jnp.bfloat16)
-            for t in z_peers:
-                where(jnp.logical_or(inner == 1, t != far), lambda: w_copy(c, t, z).start())
+            for t in z_adds:
+                w_copy(c, t, z).start()
             rsend[h, r] = weighted
             if k > 0:
                 @pl.when(it == ITERS - 1)
@@ -266,8 +265,13 @@
 
         def gradient(c, total):
             h, r = c // B, rows_y[c % B]
-            for t in z_peers:
-                where(jnp.logical_or(inner == 0, t != far), lambda: w_copy(c, t, t).wait_recv())
+            for t in z_direct:
+                w_copy(c, t, t).wait_recv()
+            if line:
+                @pl.when(inner == 0)
+                def _():
+                    for k in range(2):
+                        w_copy(c, base + k, base + k).wait_recv()
             d = d_full[pl.ds(h * W, W)]
 
             def rows(i, total):
@@ -305,13 +309,20 @@
         for p, j in group:
             g_copy(p, j, y, opt).start()
         for c in range(C):
-            for t in z_peers:
+            for t in z_direct:
                 z_copy(c, t, z).wait_send()
-                where(jnp.logical_or(inner == 1, t != far), lambda: w_copy(c, t, z).wait_send())
+            for t in z_adds:
+                w_copy(c, t, z).wait_send()
             if line:
                 @pl.when(inner == 1)
                 def _():
-                    hand_on(c).wait_send()
+                    for k in range(2):
+                        z_copy(c, base + k, z).wait_send()
+                        hand_on(c, base + k).wait_send()
+
+                @pl.when(inner == 0)
+                def _():
+                    rel_copy(c).wait_send()
         for p, j in group:
             g_copy(p, j, p, j).wait_recv()
         grad = gbuf[it, 0]
@@ -373,7 +384,7 @@
             pltpu.VMEM((C, A, R, W), f32),
             pltpu.VMEM((C, A, R, W), bf),
             pltpu.VMEM((ITERS, C, A, R, W), bf),
-            pltpu.VMEM((ITERS, C, R, W), bf),
+            pltpu.VMEM((ITERS, C, 2, R, W), bf),
             pltpu.VMEM((ITERS, C, A, R, W), bf),
             pltpu.VMEM((NH, B, R, W), f32),
             pltpu.VMEM((NH, B, R, W), f32),
@@ -384,7 +395,7 @@
             dma((NH, B)), dma((NH, B)),
             dma((3, B)), dma((3, B)),
             dma((NH, B)), dma((NH, B)),
-            dma((C, A)), dma((ITERS, C, A)), dma((ITERS, C)),
+            dma((C, A)), dma((ITERS, C, A)), dma((C,)), dma((ITERS, C)), dma((C, A)),
             dma((C, A)), dma((ITERS, C, A)),
             dma((B * NO,)), dma((ITERS, B * NO)),
             dma((4 + NH,)),

time: 128 us -> 128 us (level)
  no operation moved by 1% of the time
where the time goes in v5:
time: 128 us; the launch traced here: 127 us
  Pallas kernels  121 us (95%)
  local copies, waits for them, and re-layouts  4.56 us (4%)
    pallas_call x1, Pallas kernels, local(): pl.pallas_call(functools.partial(kernel, A, B, NO, W, pred_scale, grad_sc...  121 us
    unnamed x7, local copies, waits for them, and re-layouts  3.87 us

profile of v5, /device:TPU:0, one launch (start us, length us, event | category | flops | bytes accessed | tf_op | source)
XLA Modules:
  0.0 127.2 jit_solution(16060508070375940240)
XLA Ops:
  0.6 0.7 reshape.14.mu_in
  1.3 0.0 copy-start
  1.3 1.0 copy-done
  2.4 0.0 copy-start.1
  2.4 1.0 copy-done.1
  3.4 0.0 copy-start.2
  3.4 1.0 copy-done.2
  4.4 121.4 %shard_map.77 = (f32[1,768]{1,0:T(1,128)S(1)}, f32[128,1024]{1,0:T(8,128)S(1)}) custom-call(bf16[2,128,768]{2,1,0:T(8,128)(2,1)S(1)} %bitcast.1, bf16[1024,768]{1,0:T(8,128)(2,1)} %d_in.1, f32[128,1024]{1,0:T(8,128)S(1)} %copy-done, s32[128,1024]{1,0:T(8,128)S(1)} %copy-done.1, s32[128,1024]{1,0:T(8,128)} %class_in.1, f32[1,768]{1,0:T(1,128)S(1)} %reshape.14.mu_in), custom_call_target="tpu_custom_call" | custom-call | tf_op jit(solution)/shard_map/pallas_call | solution.py:366
  125.8 0.6 reduce
  126.4 0.8 copy.9
Async XLA Ops:
  1.3 1.0 copy-start
  2.4 1.0 copy-start.1
  3.4 1.0 copy-start.2

commit v6 on v5

--- a/solution.py
+++ b/solution.py
@@ -24,7 +24,9 @@
     q, R, X = s_in.shape
     H = d_in.shape[0] // B
     NH = H // W
-    C = NH * B
+    F = 2
+    C = NH * B * F
+    Q = R // F
     vox = lax.axis_index("vox")
     opt = lax.axis_index("opt")
     z, y = vox // B, lax.rem(vox, B)
@@ -194,9 +196,15 @@
             mine = wfull.at[it, c, src]
             return remote(mine, mine, w_send.at[c, t], w_recv.at[it, c, src], at_z(t))
 
+        def rows_of(c):
+            r, f = rows_y[c // F % B], c % F
+            return jnp.concatenate(
+                [s_full[a * B + r, pl.ds(f * Q, Q)] for a in range(A)], axis=0
+            )
+
         def predict(c):
-            h, r = c // B, rows_y[c % B]
-            if c % B == 0:
+            h, r = c // (B * F), rows_y[c // F % B]
+            if c % (B * F) == 0:
                 @pl.when(it == 0)
                 def _():
                     for p in y_peers:
@@ -205,10 +213,10 @@
                 scaled[...] = (
                     d_full[pl.ds(h * W, W)].astype(jnp.float32) * mu_ref[...]
                 ).astype(jnp.bfloat16)
-            rows = jnp.concatenate([s_full[a * B + r] for a in range(A)], axis=0)
+            rows = rows_of(c)
             part = lax.dot_general(
                 rows, scaled[...], (((1,), (1,)), ((), ())), preferred_element_type=jnp.float32
-            ).reshape(A, R, W)
+            ).reshape(A, Q, W)
             zsend[c] = part.astype(jnp.bfloat16)
             for t in z_direct:
                 z_copy(c, t, z).start()
@@ -238,9 +246,9 @@
                         hand_on(c, base + k).start()
 
         def over_z(c):
-            h, k = c // B, c % B
+            h, k, f = c // (B * F), c // F % B, c % F
             r = rows_y[k]
-            if h == 0 and k > 0:
+            if h == 0 and k > 0 and f == 0:
                 @pl.when(it == 0)
                 def _():
                     for copy in pairs(r, r)[1:]:
@@ -250,21 +258,21 @@
             for t in z_adds:
                 z_copy(c, t, t).wait_recv()
                 total = total + zrecv[it, c, t].astype(jnp.float32)
-            here = pl.ds(h * W, W)
-            code = code_ref[r, :, here].astype(jnp.float32)
+            here, part = pl.ds(h * W, W), pl.ds(f * Q, Q)
+            code = code_ref[r, part, here].astype(jnp.float32)
             weight = jnp.where(code > 0.0, 1.0 / jnp.maximum(code, 1.0), 0.0)
-            weighted = weight * (total * pred_scale - meas_ref[r, :, here])
+            weighted = weight * (total * pred_scale - meas_ref[r, part, here])
             wfull[it, c, z] = weighted.astype(jnp.bfloat16)
             for t in z_adds:
                 w_copy(c, t, z).start()
-            rsend[h, r] = weighted
-            if k > 0:
+            rsend[h, r, part] = weighted
+            if k > 0 and f == F - 1:
                 @pl.when(it == ITERS - 1)
                 def _():
                     back(h, r, y).start()
 
         def gradient(c, total):
-            h, r = c // B, rows_y[c % B]
+            h = c // (B * F)
             for t in z_direct:
                 w_copy(c, t, t).wait_recv()
             if line:
@@ -272,31 +280,26 @@
                 def _():
                     for k in range(2):
                         w_copy(c, base + k, base + k).wait_recv()
-            d = d_full[pl.ds(h * W, W)]
-
-            def rows(i, total):
-                w = wfull[it, c, pl.ds(2 * i, 2)].reshape(2 * R, W)
-                s = jnp.concatenate([s_full[(2 * i + k) * B + r] for k in range(2)], axis=0)
-                inner = jnp.dot(w, d, preferred_element_type=jnp.float32) * s.astype(jnp.float32)
-                return total + jnp.sum(inner.reshape(2 * R // 8, 8, B * X), axis=0)
-
-            return lax.fori_loop(0, A // 2, rows, total)
+            w = wfull[it, c].reshape(A * Q, W)
+            summed = jnp.dot(w, d_full[pl.ds(h * W, W)], preferred_element_type=jnp.float32)
+            summed = summed * rows_of(c).astype(jnp.float32)
+            return total + jnp.sum(summed.reshape(A * Q // 8, 8, B * X), axis=0)
 
         total = jnp.zeros((8, B * X), jnp.float32)
         for c in range(min(2, C)):
             predict(c)
         relay(0)
-        for slot in range(C + 2):
+        for slot in range(C + 3):
             if slot + 2 < C:
                 predict(slot + 2)
             if slot + 1 < C:
                 relay(slot + 1)
+            if slot < C:
+                over_z(slot)
             if 0 < slot <= C:
                 forward(slot - 1)
-            if slot < C:
-                over_z(slot)
-            if slot > 1:
-                total = gradient(slot - 2, total)
+            if slot > 2:
+                total = gradient(slot - 3, total)
 
         def g_copy(p, j, sp, sj):
             mine = gbuf.at[it, sp * NO + sj]
@@ -357,7 +360,9 @@
     H = DL // B
     W = min(H, 256)
     NH = H // W
-    C = NH * B
+    F = 2
+    C = NH * B * F
+    Q = R // F
     pred_scale = float(np.float32(1.0) / np.sqrt(np.float32(X * NV)))
     grad_scale = float(np.sqrt(np.float32(X * NV)) / np.float32(R * NV * DL * NO))
     bf, f32 = jnp.bfloat16, jnp.float32
@@ -381,11 +386,11 @@
             pltpu.VMEM((B, R, H), bf),
             pltpu.VMEM((1, B * X), f32),
             pltpu.VMEM((W, B * X), bf),
-            pltpu.VMEM((C, A, R, W), f32),
-            pltpu.VMEM((C, A, R, W), bf),
-            pltpu.VMEM((ITERS, C, A, R, W), bf),
-            pltpu.VMEM((ITERS, C, 2, R, W), bf),
-            pltpu.VMEM((ITERS, C, A, R, W), bf),
+            pltpu.VMEM((C, A, Q, W), f32),
+            pltpu.VMEM((C, A, Q, W), bf),
+            pltpu.VMEM((ITERS, C, A, Q, W), bf),
+            pltpu.VMEM((ITERS, C, 2, Q, W), bf),
+            pltpu.VMEM((ITERS, C, A, Q, W), bf),
             pltpu.VMEM((NH, B, R, W), f32),
             pltpu.VMEM((NH, B, R, W), f32),
             pltpu.VMEM((ITERS, B * NO, 1, B * X), f32),
@@ -401,7 +406,7 @@
             dma((4 + NH,)),
         ],
         compiler_params=pltpu.CompilerParams(
-            collective_id=0, has_side_effects=True, vmem_limit_bytes=52 * 1024 * 1024
+            collective_id=0, has_side_effects=True, vmem_limit_bytes=63 * 1024 * 1024
         ),
     )(
         source_fields.reshape(q, R, X), detector_fields, measured, valid_pair, weight_class,

time: 128 us -> 125 us (0.977)
  Pallas kernels: 121 us -> 119 us
  local copies, waits for them, and re-layouts: 4.56 us -> 3.15 us
    unnamed x7 -> x1, local copies, waits for them, and re-layouts: 3.87 us -> 1.88 us
    pallas_call x1, Pallas kernels: 121 us -> 119 us  [local(): pl.pallas_call(functools.partial(kernel, A, B, NO, W, pred_scale, grad_sc...]
where the time goes in v6:
time: 125 us
  Pallas kernels  119 us (95%)
  local copies, waits for them, and re-layouts  3.15 us (3%)
  other arithmetic  1.29 us (1%)
    pallas_call x1, Pallas kernels, local(): pl.pallas_call(functools.partial(kernel, A, B, NO, W, pred_scale, grad_sc...  119 us

profile of v6, /device:TPU:0, one launch (start us, length us, event | category | flops | bytes accessed | tf_op | source)
XLA Modules:
  0.0 124.5 jit_solution(11513868059268039270)
XLA Ops:
  0.6 1.3 %reshape.14.mu_in = f32[1,768]{1,0:T(1,128)} reshape(f32[768]{0:T(1024)} %param.11) | data formatting | bytes 6144 | tf_op jit(solution)/shard_map/reshape | solution.py:413
  1.9 119.4 %shard_map.77 = (f32[1,768]{1,0:T(1,128)}, f32[128,1024]{1,0:T(8,128)}) custom-call(bf16[2,128,768]{2,1,0:T(8,128)(2,1)} %bitcast.1, bf16[1024,768]{1,0:T(8,128)(2,1)} %d_in.1, f32[128,1024]{1,0:T(8,128)} %meas_in.1, s32[128,1024]{1,0:T(8,128)} %valid_in.1, s32[128,1024]{1,0:T(8,128)} %class_in.1, f32[1,768]{1,0:T(1,128)} %reshape.14.mu_in), custom_call_target="tpu_custom_call" | custom-call | tf_op jit(solution)/shard_map/pallas_call | solution.py:371
  121.3 1.3 %reduce = f32[768]{0:T(1024)} reduce(f32[1,768]{1,0:T(1,128)} %get-tuple-element.4, f32[]{:T(128)} %constant), dimensions={0}, to_apply=%get-tuple-element.4.reduce_sub_computation | reduce | bytes 6148 | tf_op jit(solution)/shard_map/pallas_call | solution.py:371
  122.6 1.9 %copy.9 = f32[128,1024]{1,0:T(8,128)} copy(f32[128,1024]{1,0:T(8,128)} %get-tuple-element.9) | data formatting | bytes 1048576

commit v7 on v6

--- a/solution.py
+++ b/solution.py
@@ -212,11 +212,9 @@
 
                 scaled[...] = (
                     d_full[pl.ds(h * W, W)].astype(jnp.float32) * mu_ref[...]
-                ).astype(jnp.bfloat16)
+                ).astype(jnp.bfloat16).T
             rows = rows_of(c)
-            part = lax.dot_general(
-                rows, scaled[...], (((1,), (1,)), ((), ())), preferred_element_type=jnp.float32
-            ).reshape(A, Q, W)
+            part = jnp.dot(rows, scaled[...], preferred_element_type=jnp.float32).reshape(A, Q, W)
             zsend[c] = part.astype(jnp.bfloat16)
             for t in z_direct:
                 z_copy(c, t, z).start()
@@ -385,7 +383,7 @@
             pltpu.VMEM((R, DL), bf),
             pltpu.VMEM((B, R, H), bf),
             pltpu.VMEM((1, B * X), f32),
-            pltpu.VMEM((W, B * X), bf),
+            pltpu.VMEM((B * X, W), bf),
             pltpu.VMEM((C, A, Q, W), f32),
             pltpu.VMEM((C, A, Q, W), bf),
             pltpu.VMEM((ITERS, C, A, Q, W), bf),

time: 125 us -> 125 us (level)
  no operation moved by 1% of the time
where the time goes in v7:
time: 125 us
  Pallas kernels  119 us (95%)
  local copies, waits for them, and re-layouts  3.15 us (3%)
  other arithmetic  1.29 us (1%)
    pallas_call x1, Pallas kernels, local(): pl.pallas_call(functools.partial(kernel, A, B, NO, W, pred_scale, grad_sc...  119 us

profile of v7, /device:TPU:0, one launch (start us, length us, event | category | flops | bytes accessed | tf_op | source)
XLA Modules:
  0.0 124.6 jit_solution(15048984199959276287)
XLA Ops:
  0.6 1.3 %reshape.14.mu_in = f32[1,768]{1,0:T(1,128)} reshape(f32[768]{0:T(1024)} %param.11) | data formatting | bytes 6144 | tf_op jit(solution)/shard_map/reshape | solution.py:411
  1.9 119.5 %shard_map.77 = (f32[1,768]{1,0:T(1,128)}, f32[128,1024]{1,0:T(8,128)}) custom-call(bf16[2,128,768]{2,1,0:T(8,128)(2,1)} %bitcast.1, bf16[1024,768]{1,0:T(8,128)(2,1)} %d_in.1, f32[128,1024]{1,0:T(8,128)} %meas_in.1, s32[128,1024]{1,0:T(8,128)} %valid_in.1, s32[128,1024]{1,0:T(8,128)} %class_in.1, f32[1,768]{1,0:T(1,128)} %reshape.14.mu_in), custom_call_target="tpu_custom_call" | custom-call | tf_op jit(solution)/shard_map/pallas_call | solution.py:369
  121.4 1.3 %reduce = f32[768]{0:T(1024)} reduce(f32[1,768]{1,0:T(1,128)} %get-tuple-element.4, f32[]{:T(128)} %constant), dimensions={0}, to_apply=%get-tuple-element.4.reduce_sub_computation | reduce | bytes 6148 | tf_op jit(solution)/shard_map/pallas_call | solution.py:369
  122.7 1.9 %copy.9 = f32[128,1024]{1,0:T(8,128)} copy(f32[128,1024]{1,0:T(8,128)} %get-tuple-element.9) | data formatting | bytes 1048576

commit v8 on v7

--- a/solution.py
+++ b/solution.py
@@ -24,7 +24,7 @@
     q, R, X = s_in.shape
     H = d_in.shape[0] // B
     NH = H // W
-    F = 2
+    F = 1
     C = NH * B * F
     Q = R // F
     vox = lax.axis_index("vox")
@@ -358,7 +358,7 @@
     H = DL // B
     W = min(H, 256)
     NH = H // W
-    F = 2
+    F = 1
     C = NH * B * F
     Q = R // F
     pred_scale = float(np.float32(1.0) / np.sqrt(np.float32(X * NV)))

time: 125 us -> 127 us (1.016)
  Pallas kernels: 119 us -> 122 us
    pallas_call x1, Pallas kernels: 119 us -> 122 us  [local(): pl.pallas_call(functools.partial(kernel, A, B, NO, W, pred_scale, grad_sc...]
where the time goes in v8:
time: 127 us
  Pallas kernels  122 us (96%)
  local copies, waits for them, and re-layouts  3.15 us (2%)
  other arithmetic  1.29 us (1%)
    pallas_call x1, Pallas kernels, local(): pl.pallas_call(functools.partial(kernel, A, B, NO, W, pred_scale, grad_sc...  122 us

profile of v8, /device:TPU:0, one launch (start us, length us, event | category | flops | bytes accessed | tf_op | source)
XLA Modules:
  0.0 126.7 jit_solution(1888288287183179920)
XLA Ops:
  0.6 1.3 %reshape.14.mu_in = f32[1,768]{1,0:T(1,128)} reshape(f32[768]{0:T(1024)} %param.11) | data formatting | bytes 6144 | tf_op jit(solution)/shard_map/reshape | solution.py:411
  1.9 121.6 %shard_map.77 = (f32[1,768]{1,0:T(1,128)}, f32[128,1024]{1,0:T(8,128)}) custom-call(bf16[2,128,768]{2,1,0:T(8,128)(2,1)} %bitcast.1, bf16[1024,768]{1,0:T(8,128)(2,1)} %d_in.1, f32[128,1024]{1,0:T(8,128)} %meas_in.1, s32[128,1024]{1,0:T(8,128)} %valid_in.1, s32[128,1024]{1,0:T(8,128)} %class_in.1, f32[1,768]{1,0:T(1,128)} %reshape.14.mu_in), custom_call_target="tpu_custom_call" | custom-call | tf_op jit(solution)/shard_map/pallas_call | solution.py:369
  123.5 1.3 %reduce = f32[768]{0:T(1024)} reduce(f32[1,768]{1,0:T(1,128)} %get-tuple-element.4, f32[]{:T(128)} %constant), dimensions={0}, to_apply=%get-tuple-element.4.reduce_sub_computation | reduce | bytes 6148 | tf_op jit(solution)/shard_map/pallas_call | solution.py:369
  124.8 1.9 %copy.9 = f32[128,1024]{1,0:T(8,128)} copy(f32[128,1024]{1,0:T(8,128)} %get-tuple-element.9) | data formatting | bytes 1048576

commit v9 on v7

--- a/solution.py
+++ b/solution.py
@@ -284,18 +284,18 @@
             return total + jnp.sum(summed.reshape(A * Q // 8, 8, B * X), axis=0)
 
         total = jnp.zeros((8, B * X), jnp.float32)
-        for c in range(min(2, C)):
+        for c in range(min(3, C)):
             predict(c)
         relay(0)
         for slot in range(C + 3):
-            if slot + 2 < C:
-                predict(slot + 2)
             if slot + 1 < C:
                 relay(slot + 1)
             if slot < C:
                 over_z(slot)
             if 0 < slot <= C:
                 forward(slot - 1)
+            if slot + 3 < C:
+                predict(slot + 3)
             if slot > 2:
                 total = gradient(slot - 3, total)
 

time: 125 us -> 125 us (level)
  no operation moved by 1% of the time
where the time goes in v9:
time: 125 us; the launch traced here: 124 us
  Pallas kernels  119 us (95%)
  local copies, waits for them, and re-layouts  3.15 us (3%)
  other arithmetic  1.29 us (1%)
    pallas_call x1, Pallas kernels, local(): pl.pallas_call(functools.partial(kernel, A, B, NO, W, pred_scale, grad_sc...  119 us

profile of v9, /device:TPU:0, one launch (start us, length us, event | category | flops | bytes accessed | tf_op | source)
XLA Modules:
  0.0 124.5 jit_solution(10204834615567547523)
XLA Ops:
  0.6 1.3 %reshape.14.mu_in = f32[1,768]{1,0:T(1,128)} reshape(f32[768]{0:T(1024)} %param.11) | data formatting | bytes 6144 | tf_op jit(solution)/shard_map/reshape | solution.py:411
  1.9 119.4 %shard_map.77 = (f32[1,768]{1,0:T(1,128)}, f32[128,1024]{1,0:T(8,128)}) custom-call(bf16[2,128,768]{2,1,0:T(8,128)(2,1)} %bitcast.1, bf16[1024,768]{1,0:T(8,128)(2,1)} %d_in.1, f32[128,1024]{1,0:T(8,128)} %meas_in.1, s32[128,1024]{1,0:T(8,128)} %valid_in.1, s32[128,1024]{1,0:T(8,128)} %class_in.1, f32[1,768]{1,0:T(1,128)} %reshape.14.mu_in), custom_call_target="tpu_custom_call" | custom-call | tf_op jit(solution)/shard_map/pallas_call | solution.py:369
  121.3 1.3 %reduce = f32[768]{0:T(1024)} reduce(f32[1,768]{1,0:T(1,128)} %get-tuple-element.4, f32[]{:T(128)} %constant), dimensions={0}, to_apply=%get-tuple-element.4.reduce_sub_computation | reduce | bytes 6148 | tf_op jit(solution)/shard_map/pallas_call | solution.py:369
  122.6 1.9 %copy.9 = f32[128,1024]{1,0:T(8,128)} copy(f32[128,1024]{1,0:T(8,128)} %get-tuple-element.9) | data formatting | bytes 1048576
